TPU v7x, 256 devices: a whole 4x4x8 slice. The times are simulated.
256 devices in a mesh: samp: 32 (over x, z), tp: 8 (over y, core).
Axes of the slice: x: 4, y: 4, z: 8, core: 2. Of those that a mesh axis runs over, the one named last changes fastest.
Arguments:
- append_states: bfloat16 [8192, 5120], P('samp'), may hold values from -6 to 6
- kv_weight: bfloat16 [5120, 2, 1024], P(None, None, 'tp'), may hold values from -0.078125 to 0.078125
- key_gain: float32 [128], replicated, may hold values from 0.1 to 1.9
- queries: bfloat16 [128, 4096], P('samp', 'tp'), may hold values from -128 to 128
- res_keys: bfloat16 [512, 128, 1024], P('samp', None, 'tp'), may hold values from -6 to 6
- res_values: bfloat16 [512, 128, 1024], P('samp', None, 'tp'), may hold values from -6 to 6
- page_table: int32 [128, 4], P('samp'), may hold values from 0 to 15, as said below
- diverge: int32 [128], replicated, may hold values from 1 to 4, as said below
- lengths: int32 [128], replicated, may hold values from 129 to 8704, as said below
- out_weight: bfloat16 [4096, 5120], P('tp'), may hold values from -0.5 to 0.5
Outputs:
- mixed: bfloat16 [128, 5120], P('samp')
Inputs may be any that keep to these rules, and one draw needn't show every extreme that they name: `page_table`: the rows of samples 4 * d to 4 * d + 3 together name every slot 0 to 15 exactly once. `diverge`: some sample has 4 and some has 1. lengths[s] - 128 * diverge[s] lies in 1 to 8192; it is 8192 for some sample with diverge 4, and 1 for some sample with diverge 1.
All inputs are finite; a program needn't handle non-finite values.
Results may differ from a plain program's by a relative error of at most 0.018.
The roundings to bfloat16 on the way count: a program that leaves them out, or rounds other values in their place, can miss the bound.
Values may be sent and summed in bfloat16 or wider, within the bound.
A program may use at most 64 MiB of HBM per device.

v0:
```python
import jax
import jax.numpy as jnp
from jax import lax
from jax.sharding import PartitionSpec as P

ROPE_BASE = 1000000.0
NORM_EPS = 1e-06
FLOOR = -1e30


def rotate(vectors, positions):
    half_width = vectors.shape[-1] // 2
    frequency = ROPE_BASE ** (
        -(jnp.arange(half_width, dtype=jnp.float32) * 2.0 / vectors.shape[-1])
    )
    angles = positions.astype(jnp.float32)[..., None] * frequency
    cosine = jnp.cos(angles)
    sine_part = jnp.sin(angles)
    first_part = vectors[..., :half_width]
    second_part = vectors[..., half_width:]
    return jnp.concatenate(
        [
            first_part * cosine - second_part * sine_part,
            second_part * cosine + first_part * sine_part,
        ],
        axis=-1,
    )


def partial_softmax(query_rows, key_rows, value_rows, valid_keys):
    shared = key_rows.ndim == 3
    score_form = "skgd,tkd->skgt" if shared else "skgd,stkd->skgt"
    value_form = "skgt,tkd->skgd" if shared else "skgt,stkd->skgd"
    scores = jnp.einsum(
        score_form, query_rows, key_rows, preferred_element_type=jnp.float32
    ) * query_rows.shape[-1] ** (-0.5)
    key_mask = valid_keys[:, None, None, :]
    highest = jnp.max(jnp.where(key_mask, scores, FLOOR), axis=-1)
    weights = jnp.where(key_mask, jnp.exp(scores - highest[..., None]), 0.0)
    totals = jnp.sum(weights, axis=-1)
    summed = jnp.einsum(
        value_form, weights.astype(jnp.bfloat16), value_rows, preferred_element_type=jnp.float32
    )
    return (highest, totals, summed)


def combine(first_part, second_part):
    running_max = jnp.maximum(first_part[0], second_part[0])
    scale_first = jnp.exp(first_part[0] - running_max)
    scale_second = jnp.exp(second_part[0] - running_max)
    totals = first_part[1] * scale_first + second_part[1] * scale_second
    summed = first_part[2] * scale_first[..., None] + second_part[2] * scale_second[..., None]
    return (running_max, totals, summed)


def local(
    append_states,
    kv_weight,
    key_gain,
    queries,
    res_keys,
    res_values,
    page_table,
    diverge,
    lengths,
    out_weight,
):
    head_dim = key_gain.shape[0]
    app_rows = append_states.shape[0]
    local_kv = kv_weight.shape[2] // head_dim
    sample_rows = queries.shape[0]
    local_heads = queries.shape[1] // head_dim
    group_size = local_heads // local_kv
    page_rows = res_keys.shape[1]
    owner_index = lax.axis_index("samp")
    projected = jnp.dot(
        append_states, kv_weight.reshape(kv_weight.shape[0], -1), preferred_element_type=jnp.float32
    ).reshape(app_rows, 2, local_kv, head_dim)
    raw_keys = projected[:, 0]
    key_scale = lax.rsqrt(jnp.mean(raw_keys * raw_keys, axis=-1, keepdims=True) + NORM_EPS)
    app_positions = owner_index * app_rows + jnp.arange(app_rows, dtype=jnp.int32)
    app_keys = rotate(raw_keys * key_scale * key_gain, app_positions[:, None]).astype(jnp.bfloat16)
    app_values = projected[:, 1].astype(jnp.bfloat16)
    first_sample = owner_index * sample_rows
    my_lengths = lax.dynamic_slice_in_dim(lengths, first_sample, sample_rows)
    my_diverge = lax.dynamic_slice_in_dim(diverge, first_sample, sample_rows)
    my_used = my_lengths - page_rows * my_diverge
    query_heads = queries.astype(jnp.float32).reshape(sample_rows, local_heads, head_dim)
    query_res = (
        rotate(query_heads, my_lengths[:, None])
        .astype(jnp.bfloat16)
        .reshape(sample_rows, local_kv, group_size, head_dim)
    )
    query_app = (
        rotate(query_heads, my_used[:, None])
        .astype(jnp.bfloat16)
        .reshape(sample_rows, local_kv, group_size, head_dim)
    )
    slot_keys = res_keys[page_table].reshape(sample_rows, -1, local_kv, head_dim)
    slot_values = res_values[page_table].reshape(sample_rows, -1, local_kv, head_dim)
    context_rows = slot_keys.shape[1]
    resident_valid = (
        jnp.arange(context_rows, dtype=jnp.int32)[None, :] < (page_rows * my_diverge)[:, None]
    )
    resident = partial_softmax(query_res, slot_keys, slot_values, resident_valid)
    starting = (
        jnp.full((sample_rows, local_kv, group_size), FLOOR, jnp.float32),
        jnp.zeros((sample_rows, local_kv, group_size), jnp.float32),
        jnp.zeros((sample_rows, local_kv, group_size, head_dim), jnp.float32),
    )
    pieces = (
        lax.all_gather(app_keys, "samp", axis=0, tiled=True),
        lax.all_gather(app_values, "samp", axis=0, tiled=True),
    )
    piece_rows = pieces[0].shape[0]
    piece_valid = jnp.arange(piece_rows, dtype=jnp.int32)[None, :] < my_used[:, None]
    appended = combine(starting, partial_softmax(query_app, pieces[0], pieces[1], piece_valid))
    running_max, totals, summed = combine(resident, appended)
    attended = (
        (summed / totals[..., None])
        .reshape(sample_rows, local_heads * head_dim)
        .astype(jnp.bfloat16)
    )
    partial_out = jnp.dot(attended, out_weight, preferred_element_type=jnp.float32)
    return lax.psum(partial_out.astype(jnp.bfloat16), "tp")


def solution(mesh):
    return jax.shard_map(
        local,
        mesh=mesh,
        in_specs=(
            P("samp", None),
            P(None, None, "tp"),
            P(),
            P("samp", "tp"),
            P("samp", None, "tp"),
            P("samp", None, "tp"),
            P("samp", None),
            P(),
            P(),
            P("tp", None),
        ),
        out_specs=P("samp", None),
        check_vma=False,
    )
```

profile of v0, /device:TPU:1, one launch (start us, length us, event | category | flops | bytes accessed | tf_op | source)
XLA Modules:
  0.0 208.7 jit_solution(15503258790639405375)
XLA Ops:
  6.6 3.7 %copy.25 = bf16[640,8,2,128]{3,1,2,0:T(8,128)(2,1)} copy(bf16[640,8,2,128]{3,2,1,0:T(2,128)(2,1)} %bitcast.86) | data formatting | bytes 5242880
  10.3 4.4 %copy.11 = bf16[256,5120]{1,0:T(8,128)(2,1)} copy(bf16[256,5120]{0,1:T(8,128)(2,1)} %bitcast.85) | data formatting | bytes 5242880 | tf_op jit(solution)/shard_map/dot_general | solution.py:76
  14.7 2.6 %fusion.6 = f32[256,2,1,128]{0,3,1,2:T(8,128)S(1)} fusion(bf16[2,128,5120]{2,1,0:T(8,128)(2,1)} %bitcast.87, bf16[256,5120]{1,0:T(8,128)(2,1)S(1)} %copy-done), kind=kOutput, calls=%fused_computation.11 | convolution fusion | flops 671088640 | bytes 5505024 | tf_op jit(solution)/shard_map/dot_general | solution.py:76
  17.5 0.1 multiply_multiply_fusion
  17.6 0.3 fusion.41
  17.9 0.6 pad_maximum_fusion
  18.6 0.6 slice.55
  19.3 0.1 reshape.550
  19.4 1.7 gather_fusion
  21.1 2.5 %gather_fusion.1 = bf16[16,128,128]{2,1,0:T(8,128)(2,1)} fusion(bf16[16,128,128]{2,1,0:T(8,128)(2,1)} %param.15, s32[1024]{0:T(1024)S(1)} %pad_clamp_fusion), kind=kCustom, calls=%fused_computation.1 | custom fusion | bytes 1048640 | tf_op jit(solution)/shard_map/gather | solution.py:100
  23.7 0.1 multiply_cosine_fusion.2
  23.9 0.1 subtract_convert_fusion.1
  24.0 0.4 select_reduce_fusion.1
  24.3 0.2 fusion.44
  24.5 0.1 iota_compare_fusion
  24.6 69.6 %all-gather.4.cloned.1.call-done = bf16[8192,1,128]{0,2,1:T(8,128)(2,1)} async-done(((bf16[256,1,128]{0,2,1:T(8,128)(2,1)}), bf16[8192,1,128]{0,2,1:T(8,128)(2,1)}) %all-gather.4.cloned.1.call-update) | async-done | bytes 2097168 | tf_op jit(solution)/shard_map/all_gather | solution.py:112
  94.2 2.3 %select_reduce_fusion = (f32[4,4]{1,0:T(4,128)S(1)}, f32[4,1,4,8192]{3,2,0,1:T(4,128)S(1)}) fusion(pred[4,8192]{1,0:T(4,128)(4,1)S(1)} %iota_compare_fusion, bf16[4,4,64]{2,1,0:T(4,128)(2,1)S(1)} %get-tuple-element.16, bf16[4,4,64]{2,1,0:T(4,128)(2,1)S(1)} %get-tuple-element.17, bf16[8192,1,128]{0,2,1:T(8,128)(2,1)} %all-gather.4.cloned.1.call-done), kind=kOutput, calls=%fused_computation.25 | convolution fusion | flops 33955824 | bytes 2658368 | tf_op jit(solution)/shard_map/skgd,tkd->skgt/dot_general | solution.py:34
  96.5 0.8 copy-done.2
  97.3 0.4 fusion.29
  97.7 73.1 %all-gather.6.cloned.1.call-done = bf16[8192,1,1,128]{0,3,1,2:T(8,128)(2,1)} async-done(((bf16[256,1,1,128]{0,3,1,2:T(8,128)(2,1)}), bf16[8192,1,1,128]{0,3,1,2:T(8,128)(2,1)}) %all-gather.6.cloned.1.call-update) | async-done | bytes 2097168 | tf_op jit(solution)/shard_map/all_gather | solution.py:113
  170.8 2.5 %fusion.25 = f32[4,1,4,128]{3,2,0,1:T(4,128)S(1)} fusion(bf16[8192,1,1,128]{0,3,1,2:T(8,128)(2,1)} %all-gather.6.cloned.1.call-done, f32[4,1,4,8192]{3,2,0,1:T(4,128)} %copy-done.2, f32[4,4]{1,0:T(4,128)S(1)} %get-tuple-element.31, pred[4,8192]{1,0:T(4,128)(4,1)S(1)} %iota_compare_fusion, f32[4,4]{1,0:T(4,128)S(1)} %get-tuple-element.21, ...), kind=kOutput, calls=%fused_computation.22 | convolution fusion | flops 33953792 | bytes 2662656 | tf_op jit(solution)/shard_map/skgt,tkd->skgd/dot_general | solution.py:41
  173.3 0.2 fusion.28
  173.5 3.3 %convolution_convert_fusion = bf16[4,5120]{1,0:T(4,128)(2,1)S(1)} fusion(bf16[512,5120]{1,0:T(8,128)(2,1)} %param.19, bf16[1,4,4,128]{3,2,1,0:T(4,128)(2,1)S(1)} %fusion.28), kind=kOutput, calls=%fused_computation.4 | convolution fusion | flops 20992000 | bytes 5287936 | tf_op jit(solution)/shard_map/dot_general | solution.py:124
  176.8 25.1 %psum.7 = bf16[4,5120]{1,0:T(4,128)(2,1)} all-reduce(bf16[4,5120]{1,0:T(4,128)(2,1)S(1)} %convolution_convert_fusion), channel_id=1, replica_groups=mesh['samp'=32,'tp'=8] {'tp'}, use_global_device_ids=true, to_apply=%region_5.6 | all-reduce | flops 20480 | bytes 81920 | tf_op jit(solution)/shard_map/psum | solution.py:125
  (29 shorter events, 0.4 us)
Async XLA Ops:
  6.5 8.2 %copy-start = (bf16[256,5120]{1,0:T(8,128)(2,1)S(1)}, bf16[256,5120]{1,0:T(8,128)(2,1)}, u32[]{:S(2)}) copy-start(bf16[256,5120]{1,0:T(8,128)(2,1)} %param.10) | copy-start | bytes 7864324
  6.5 87.7 %all-gather.4.cloned.1.call-start = ((), (), s32[]{:S(2)}) async-start(), calls=%async_computation | async-start | bytes 2162688 | tf_op jit(solution)/shard_map/all_gather | solution.py:112
  14.7 2.8 %copy-start.5 = (f32[128]{0:T(128)S(1)}, f32[128]{0:T(128)}, u32[]{:S(2)}) copy-start(f32[128]{0:T(128)} %param.12) | copy-start | bytes 1540
  14.7 4.6 %copy-start.3 = (bf16[4,512]{1,0:T(4,128)(2,1)S(1)}, bf16[4,512]{1,0:T(4,128)(2,1)}, u32[]{:S(2)}) copy-start(bf16[4,512]{1,0:T(4,128)(2,1)} %param.13) | copy-start | bytes 12292
  14.7 4.6 %copy-start.4 = (s32[4,4]{1,0:T(4,128)S(1)}, s32[4,4]{1,0:T(4,128)}, u32[]{:S(2)}) copy-start(s32[4,4]{1,0:T(4,128)} %param.16) | copy-start | bytes 196
  17.4 6.2 %copy-start.6 = (s32[128]{0:T(128)S(1)}, s32[128]{0:T(128)}, u32[]{:S(2)}) copy-start(s32[128]{0:T(128)} %param.17) | copy-start | bytes 1540
  17.4 6.2 %copy-start.7 = (s32[128]{0:T(128)S(1)}, s32[128]{0:T(128)}, u32[]{:S(2)}) copy-start(s32[128]{0:T(128)} %param.18) | copy-start | bytes 1540
  18.5 152.2 %all-gather.6.cloned.1.call-start = ((), (), s32[]{:S(2)}) async-start(), calls=%async_computation.1 | async-start | bytes 2162688 | tf_op jit(solution)/shard_map/all_gather | solution.py:113
  96.5 0.8 copy-start.2
  96.5 76.8 %copy-start.1 = (bf16[16,128,128]{2,1,0:T(8,128)(2,1)S(1)}, bf16[16,128,128]{2,1,0:T(8,128)(2,1)}, u32[]{:S(2)}) copy-start(bf16[16,128,128]{2,1,0:T(8,128)(2,1)} %gather_fusion.1) | copy-start | bytes 1572868
Sparse Core Ops, SparseCore 0:
  18.7 75.4 all-gather.3
  96.7 74.0 all-gather.5
where the time goes:
time: 211 us; the launch traced here: 209 us
  waiting for transfers between devices  143 us (68%)
  blocking collectives  25.1 us (12%)
  local copies, waits for them, and re-layouts  13.9 us (7%)
  between operations  13.6 us (6%)
  matrix products  11.3 us (5%)
  other arithmetic  2.18 us (1%)
    all_gather x1, waiting for transfers between devices, local(): lax.all_gather(app_values, 'samp', axis=0, tiled=True)  73.1 us
    all_gather x1, waiting for transfers between devices, local(): lax.all_gather(app_keys, 'samp', axis=0, tiled=True)  69.6 us
    psum x1, blocking collectives, local(): return lax.psum(partial_out.astype(jnp.bfloat16), 'tp')  25.1 us
    unnamed x17, local copies, waits for them, and re-layouts  4.56 us
    dot_general x1, local copies, waits for them, and re-layouts, local(): jnp.dot(append_states, kv_weight.reshape(kv_weight.shape[0], -1), preferr...  4.43 us
  transfers between devices with their start and end apart: 2, of which 2 were waited for; matrix products, arithmetic and copies ran while one was open for 4% of the time, Pallas kernels for 0%

commit v1 on v0

v1 whole, which is shorter than its diff:
```python
import numpy as np
import jax
import jax.numpy as jnp
from jax import lax
from jax.experimental import pallas as pl
from jax.experimental.pallas import tpu as pltpu
from jax.sharding import PartitionSpec as P

ROPE_BASE = 1000000.0
NORM_EPS = 1e-06
FLOOR = -1e30
S = 32
T = 8
HD = 128
D = 5120
ROWS = 256
NC = 5
DC = D // NC
COLS = D // T
MESH = pl.DeviceIdType.MESH

COS0, SIN0, COSB, SINB, FREQ = 0, 256, 512, 544, 576


def rope_table():
    freq = ROPE_BASE ** (-(np.arange(64, dtype=np.float64) * 2.0 / HD))
    freq = np.concatenate([freq, freq])
    row = np.arange(ROWS, dtype=np.float64)[:, None] * freq
    base = (np.arange(S, dtype=np.float64) * ROWS)[:, None] * freq
    last = np.zeros((8, HD))
    last[:] = freq
    return np.concatenate([np.cos(row), np.sin(row), np.cos(base), np.sin(base), last]).astype(
        np.float32
    )


def swap_halves(v):
    lane = lax.broadcasted_iota(jnp.int32, v.shape, 1)
    return jnp.where(lane < 64, -1.0, 1.0) * pltpu.roll(v, 64, 1)


def kernel(
    x_hbm,
    w_hbm,
    gain_hbm,
    q_hbm,
    rk_hbm,
    rv_hbm,
    pt_hbm,
    div_hbm,
    len_hbm,
    ow_hbm,
    tab_hbm,
    out_ref,
    x_v,
    w_v,
    wd,
    gain_v,
    q_v,
    rk_v,
    rv_v,
    pt_s,
    div_s,
    len_s,
    div_v,
    len_v,
    ow_v,
    tab_v,
    q_send,
    q_res,
    q_all,
    o_send,
    o_all,
    st_send,
    st_all,
    tr_v,
    rs_send,
    rs_all,
    ag,
    small_sem,
    chunk_sem,
    page_sem,
    ow_sem,
    send_sem,
    recv_sem,
):
    me = lax.axis_index("samp")
    mt = lax.axis_index("tp")

    small = [
        pltpu.make_async_copy(src, dst, small_sem.at[i])
        for i, (src, dst) in enumerate(
            [
                (len_hbm, len_s),
                (div_hbm, div_s),
                (q_hbm, q_v),
                (tab_hbm, tab_v),
                (pt_hbm, pt_s),
                (len_hbm, len_v),
                (div_hbm, div_v),
                (gain_hbm, gain_v),
            ]
        )
    ]
    for copy in small:
        copy.start()
    w_copies = [
        pltpu.make_async_copy(
            w_hbm.at[pl.ds(c * 2 * DC, 2 * DC)], w_v.at[pl.ds(c * 2 * DC, 2 * DC)], chunk_sem.at[0, c]
        )
        for c in range(NC)
    ]
    x_copies = [
        pltpu.make_async_copy(
            x_hbm.at[:, pl.ds(c * DC, DC)], x_v.at[:, pl.ds(c * DC, DC)], chunk_sem.at[1, c]
        )
        for c in range(NC)
    ]
    for c in range(NC):
        w_copies[c].start()
        x_copies[c].start()
    pages = [
        pltpu.make_async_copy(rk_hbm, rk_v, page_sem.at[0]),
        pltpu.make_async_copy(rv_hbm, rv_v, page_sem.at[1]),
    ]
    for copy in pages:
        copy.start()
    ow_copy = pltpu.make_async_copy(ow_hbm, ow_v, ow_sem)
    ow_copy.start()

    barrier = pltpu.get_barrier_semaphore()

    @pl.loop(1, S)
    def _(k):
        pl.semaphore_signal(
            barrier, inc=1, device_id={"samp": lax.rem(me + k, S)}, device_id_type=MESH
        )

    @pl.loop(1, T)
    def _(k):
        pl.semaphore_signal(
            barrier, inc=1, device_id={"tp": lax.rem(mt + k, T)}, device_id_type=MESH
        )

    for copy in small:
        copy.wait()
    row = lax.broadcasted_iota(jnp.int32, (16, HD), 0)
    sample = lax.rem(row, 4)

    def by_sample(values):
        return jnp.where(
            sample == 0,
            values[0],
            jnp.where(sample == 1, values[1], jnp.where(sample == 2, values[2], values[3])),
        )

    my_len = [len_s[0, me * 4 + i] for i in range(4)]
    my_div = [div_s[0, me * 4 + i] for i in range(4)]
    freq = tab_v[FREQ : FREQ + 1, :]
    q = q_v[...].astype(jnp.float32)
    q = jnp.concatenate([q[:, h * HD : (h + 1) * HD] for h in range(4)], axis=0)
    q_swapped = swap_halves(q)

    def rotate(positions):
        angle = by_sample(positions).astype(jnp.float32) * freq
        return (q * jnp.cos(angle) + q_swapped * jnp.sin(angle)).astype(jnp.bfloat16)

    q_app = rotate([my_len[i] - 128 * my_div[i] for i in range(4)])
    q_res[...] = rotate(my_len)
    q_send[...] = q_app
    q_all[me] = q_app

    pl.semaphore_wait(barrier, S - 1 + T - 1)

    @pl.loop(1, S)
    def _(k):
        pltpu.make_async_remote_copy(
            src_ref=q_send,
            dst_ref=q_all.at[me],
            send_sem=send_sem.at[0],
            recv_sem=recv_sem.at[0],
            device_id={"samp": lax.rem(me + k, S)},
            device_id_type=MESH,
        ).start()

    used = len_v[...] - 128 * div_v[...]
    high = lax.shift_right_logical(used, 7)
    low = used - 128 * high
    pair_row = lax.broadcasted_iota(jnp.int32, (16, 128), 0)
    pair = jnp.where(pair_row == 0, high, jnp.where(pair_row == 1, low, 0))
    e_row = lax.broadcasted_iota(jnp.int32, (128, 512), 0)
    e_col = lax.broadcasted_iota(jnp.int32, (128, 512), 1)
    spread = jnp.where(
        e_row == 4 * lax.shift_right_logical(e_col, 4) + jnp.bitwise_and(e_col, 3), 1.0, 0.0
    ).astype(jnp.bfloat16)
    wide = jnp.dot(
        pair.astype(jnp.float32).astype(jnp.bfloat16), spread, preferred_element_type=jnp.float32
    )
    used_wide = (wide[0:1] * 128.0 + wide[1:2]).astype(jnp.int32)

    p_row = lax.broadcasted_iota(jnp.int32, (256, 256), 0)
    p_col = lax.broadcasted_iota(jnp.int32, (256, 256), 1)
    perm = jnp.where(
        p_col == jnp.where(p_row < 128, 2 * p_row, 2 * p_row - 255), 1.0, 0.0
    ).astype(jnp.bfloat16)
    acc = jnp.zeros((ROWS, 256), jnp.float32)
    for c in range(NC):
        w_copies[c].wait()
        for i in range(c * DC // 256, (c + 1) * DC // 256):
            pairs = jnp.concatenate(
                [w_v[pl.ds(i * 512, 256), :], w_v[pl.ds(i * 512 + 256, 256), :]], axis=1
            )
            apart = jnp.dot(perm, pairs, preferred_element_type=jnp.float32).astype(jnp.bfloat16)
            wd[pl.ds(i * 256, 128), 0:128] = apart[0:128, 0:128]
            wd[pl.ds(i * 256, 128), 128:256] = apart[128:256, 0:128]
            wd[pl.ds(i * 256 + 128, 128), 0:128] = apart[0:128, 128:256]
            wd[pl.ds(i * 256 + 128, 128), 128:256] = apart[128:256, 128:256]
        x_copies[c].wait()
        acc = acc + jnp.dot(
            x_v[:, c * DC : (c + 1) * DC],
            wd[c * DC : (c + 1) * DC, :],
            preferred_element_type=jnp.float32,
        )
    raw = acc[:, 0:128]
    values = acc[:, 128:256].astype(jnp.bfloat16)
    scale = lax.rsqrt(jnp.mean(raw * raw, axis=1, keepdims=True) + NORM_EPS)
    keys = raw * scale * gain_v[...]
    cos_b = tab_v[pl.ds(COSB + me, 1), :]
    sin_b = tab_v[pl.ds(SINB + me, 1), :]
    cos_0 = tab_v[COS0 : COS0 + ROWS, :]
    sin_0 = tab_v[SIN0 : SIN0 + ROWS, :]
    cos = cos_0 * cos_b - sin_0 * sin_b
    sin = sin_0 * cos_b + cos_0 * sin_b
    keys = (keys * cos + swap_halves(keys) * sin).astype(jnp.bfloat16)

    pltpu.make_async_copy(
        q_all.at[pl.ds(0, S - 1)], q_all.at[pl.ds(0, S - 1)], recv_sem.at[0]
    ).wait()
    scores = lax.dot_general(
        keys,
        q_all[...].reshape(S * 16, HD),
        (((1,), (1,)), ((), ())),
        preferred_element_type=jnp.float32,
    ) * (HD**-0.5)
    position = lax.broadcasted_iota(jnp.int32, (ROWS, S * 16), 0) + me * ROWS
    valid = position < used_wide
    top = jnp.max(jnp.where(valid, scores, FLOOR), axis=0, keepdims=True)
    weights = jnp.where(valid, jnp.exp(scores - top), 0.0)
    total = jnp.sum(weights, axis=0, keepdims=True)
    part = lax.dot_general(
        weights.astype(jnp.bfloat16),
        values,
        (((0,), (0,)), ((), ())),
        preferred_element_type=jnp.float32,
    )
    o_send[...] = part.astype(jnp.bfloat16).reshape(S, 16, HD)
    for g in range(4):
        st_send[g, 0:1, :] = top[:, g * 128 : (g + 1) * 128]
        st_send[g, 1:2, :] = total[:, g * 128 : (g + 1) * 128]

    @pl.loop(1, S)
    def _(k):
        peer = lax.rem(me + k, S)
        pltpu.make_async_remote_copy(
            src_ref=o_send.at[peer],
            dst_ref=o_all.at[me],
            send_sem=send_sem.at[1],
            recv_sem=recv_sem.at[1],
            device_id={"samp": peer},
            device_id_type=MESH,
        ).start()
        pltpu.make_async_remote_copy(
            src_ref=st_send.at[peer // 8],
            dst_ref=st_all.at[me],
            send_sem=send_sem.at[2],
            recv_sem=recv_sem.at[2],
            device_id={"samp": peer},
            device_id_type=MESH,
        ).start()

    o_all[me] = o_send[me]
    st_all[me] = st_send[me // 8]

    for copy in pages:
        copy.wait()
    lane = lax.broadcasted_iota(jnp.int32, (16, HD), 1)
    slot_ok = jnp.zeros((16, HD), jnp.float32)
    for j in range(4):
        page = by_sample([pt_s[i, j] for i in range(4)])
        count = by_sample(my_div)
        slot_ok = jnp.where((lane == page) & (count > j), 1.0, slot_ok)
    seen = jnp.concatenate(
        [jnp.broadcast_to(slot_ok[:, k : k + 1], (16, HD)) for k in range(16)], axis=1
    ) > 0.5
    res_scores = lax.dot_general(
        q_res[...], rk_v[...], (((1,), (1,)), ((), ())), preferred_element_type=jnp.float32
    ) * (HD**-0.5)
    res_top = jnp.max(jnp.where(seen, res_scores, FLOOR), axis=1, keepdims=True)
    res_weights = jnp.where(seen, jnp.exp(res_scores - res_top), 0.0)
    res_total = jnp.sum(res_weights, axis=1, keepdims=True)
    res_part = jnp.dot(
        res_weights.astype(jnp.bfloat16), rv_v[...], preferred_element_type=jnp.float32
    )

    pltpu.make_async_copy(
        st_all.at[pl.ds(0, S - 1)], st_all.at[pl.ds(0, S - 1)], recv_sem.at[2]
    ).wait()
    pltpu.make_async_copy(
        o_all.at[pl.ds(0, S - 1)], o_all.at[pl.ds(0, S - 1)], recv_sem.at[1]
    ).wait()
    tops = jnp.concatenate([st_all[:, 0, :], jnp.full((128 - S, 128), FLOOR, jnp.float32)], axis=0)
    totals = jnp.concatenate([st_all[:, 1, :], jnp.zeros((128 - S, 128), jnp.float32)], axis=0)
    tr_v[0] = tops.T
    tr_v[1] = totals.T
    mine = pl.multiple_of(16 * lax.rem(me, 8), 16)
    tops = tr_v[0, pl.ds(mine, 16), :]
    totals = tr_v[1, pl.ds(mine, 16), :]
    highest = jnp.maximum(jnp.max(tops, axis=1, keepdims=True), res_top)
    factor = jnp.exp(tops - highest)
    res_factor = jnp.exp(res_top - highest)
    whole = jnp.sum(factor * totals, axis=1, keepdims=True) + res_factor * res_total
    attended = res_part * res_factor
    for i in range(S):
        attended = attended + factor[:, i : i + 1] * o_all[i].astype(jnp.float32)
    attended = attended / whole
    attended = jnp.concatenate(
        [attended if h == 0 else pltpu.roll(attended, 16 - 4 * h, 0) for h in range(4)], axis=1
    ).astype(jnp.bfloat16)

    ow_copy.wait()

    @pl.loop(1, T)
    def _(k):
        peer = lax.rem(mt + k, T)
        columns = pl.ds(pl.multiple_of(peer * COLS, COLS), COLS)
        piece = jnp.dot(attended, ow_v[:, columns], preferred_element_type=jnp.float32)
        rs_send[peer] = piece[0:4, :]
        pltpu.make_async_remote_copy(
            src_ref=rs_send.at[peer],
            dst_ref=rs_all.at[mt],
            send_sem=send_sem.at[3],
            recv_sem=recv_sem.at[3],
            device_id={"tp": peer},
            device_id_type=MESH,
        ).start()

    columns = pl.ds(pl.multiple_of(mt * COLS, COLS), COLS)
    rs_all[mt] = jnp.dot(attended, ow_v[:, columns], preferred_element_type=jnp.float32)[0:4, :]
    pltpu.make_async_copy(
        rs_all.at[pl.ds(0, T - 1)], rs_all.at[pl.ds(0, T - 1)], recv_sem.at[3]
    ).wait()
    piece = rs_all[0]
    for t in range(1, T):
        piece = piece + rs_all[t]
    ag[mt] = piece

    @pl.loop(1, T)
    def _(k):
        pltpu.make_async_remote_copy(
            src_ref=ag.at[mt],
            dst_ref=ag.at[mt],
            send_sem=send_sem.at[4],
            recv_sem=recv_sem.at[4],
            device_id={"tp": lax.rem(mt + k, T)},
            device_id_type=MESH,
        ).start()

    pltpu.make_async_copy(
        ag.at[pl.ds(0, T - 1)], ag.at[pl.ds(0, T - 1)], recv_sem.at[4]
    ).wait()
    for t in range(T):
        out_ref[:, t * COLS : (t + 1) * COLS] = ag[t].astype(jnp.bfloat16)

    for sem, buffer, n in ((0, q_all, S), (1, o_all, S), (2, st_all, S), (3, rs_all, T), (4, ag, T)):
        part_ref = buffer.at[pl.ds(0, n - 1)]
        pltpu.make_async_copy(part_ref, part_ref, send_sem.at[sem]).wait()


def local(x, w, gain, q, rk, rv, pt, div, length, ow):
    bf16, f32, i32 = jnp.bfloat16, jnp.float32, jnp.int32
    hbm = pl.BlockSpec(memory_space=pl.ANY)
    V = pltpu.VMEM
    return pl.pallas_call(
        kernel,
        out_shape=jax.ShapeDtypeStruct((4, D), bf16),
        in_specs=[hbm] * 11,
        out_specs=pl.BlockSpec(memory_space=pltpu.VMEM),
        scratch_shapes=[
            V((ROWS, D), bf16),
            V((2 * D, HD), bf16),
            V((D, 256), bf16),
            V((1, HD), f32),
            V((4, 512), bf16),
            V((2048, HD), bf16),
            V((2048, HD), bf16),
            pltpu.SMEM((4, 4), i32),
            pltpu.SMEM((1, 128), i32),
            pltpu.SMEM((1, 128), i32),
            V((1, 128), i32),
            V((1, 128), i32),
            V((512, D), bf16),
            V((584, HD), f32),
            V((16, HD), bf16),
            V((16, HD), bf16),
            V((S, 16, HD), bf16),
            V((S, 16, HD), bf16),
            V((S, 16, HD), bf16),
            V((4, 2, 128), f32),
            V((S, 2, 128), f32),
            V((2, 128, 128), f32),
            V((T, 4, COLS), f32),
            V((T, 4, COLS), f32),
            V((T, 4, COLS), f32),
            pltpu.SemaphoreType.DMA((8,)),
            pltpu.SemaphoreType.DMA((2, NC)),
            pltpu.SemaphoreType.DMA((2,)),
            pltpu.SemaphoreType.DMA,
            pltpu.SemaphoreType.DMA((5,)),
            pltpu.SemaphoreType.DMA((5,)),
        ],
        compiler_params=pltpu.CompilerParams(
            collective_id=0, has_side_effects=True, vmem_limit_bytes=40 * 1024 * 1024
        ),
        cost_estimate=pl.CostEstimate(
            flops=1_500_000_000, bytes_accessed=12_000_000, transcendentals=200_000
        ),
    )(
        x,
        w.reshape(2 * D, HD),
        gain.reshape(1, HD),
        q,
        rk.reshape(2048, HD),
        rv.reshape(2048, HD),
        pt,
        div.reshape(1, 128),
        length.reshape(1, 128),
        ow,
        jnp.asarray(rope_table()),
    )


def solution(mesh):
    return jax.shard_map(
        local,
        mesh=mesh,
        in_specs=(
            P("samp", None),
            P(None, None, "tp"),
            P(),
            P("samp", "tp"),
            P("samp", None, "tp"),
            P("samp", None, "tp"),
            P("samp", None),
            P(),
            P(),
            P("tp", None),
        ),
        out_specs=P("samp", None),
        check_vma=False,
    )
```

time: 211 us -> 49.4 us (0.23)
  waiting for transfers between devices: 143 us -> 0 us
  Pallas kernels: 0 us -> 36 us
  blocking collectives: 25.1 us -> 0 us
  between operations: 13.6 us -> 0.02 us
  matrix products: 11.3 us -> 0 us
  other arithmetic: 2.18 us -> 0 us
    all_gather x2 -> x0, waiting for transfers between devices: 143 us -> none  [the longest x1 73.1 us: local(): lax.all_gather(app_values, 'samp', axis=0, tiled=True)]
    pallas_call x0 -> x1, Pallas kernels: none -> 36 us  [local(): pl.pallas_call(kernel, out_shape=jax.ShapeDtypeStruct((4, D), bf16), in_s...]
    psum x1 -> x0, blocking collectives: 25.1 us -> none  [local(): return lax.psum(partial_out.astype(jnp.bfloat16), 'tp')]
    dot_general x6 -> x0, matrix products: 11.3 us -> none  [the longest x1 3.28 us: local(): jnp.dot(attended, out_weight, preferred_element_type=jnp.float32)]
    unnamed x17 -> x23, local copies, waits for them, and re-layouts: 4.56 us -> 13 us
    dot_general x1 -> x0, local copies, waits for them, and re-layouts: 4.43 us -> none  [local(): jnp.dot(append_states, kv_weight.reshape(kv_weight.shape[0], -1), preferr...]
    gather x2 -> x0, local copies, waits for them, and re-layouts: 4.15 us -> none  [the longest x1 2.46 us: local(): res_values[page_table].reshape(sample_rows, -1, local_kv, head_dim)]
  transfers between devices with their start and end apart: 2 -> 0, of which waited for: 2 -> 0; matrix products, arithmetic and copies ran while one was open for 4% -> 0% of each run, Pallas kernels for 0% -> 0%
where the time goes in v1:
time: 49.4 us; the launch traced here: 49 us
  Pallas kernels  36 us (73%)
  local copies, waits for them, and re-layouts  13 us (26%)
    pallas_call x1, Pallas kernels, local(): pl.pallas_call(kernel, out_shape=jax.ShapeDtypeStruct((4, D), bf16), in_s...  36 us
    unnamed x23, local copies, waits for them, and re-layouts  13 us

profile of v1, /device:TPU:1, one launch (start us, length us, event | category | flops | bytes accessed | tf_op | source)
XLA Modules:
  0.0 49.0 jit_solution(5903053221945839302)
XLA Ops:
  0.0 0.0 copy-start
  0.0 2.5 %copy-done = bf16[512,5120]{1,0:T(8,128)(2,1)S(1)} copy-done((bf16[512,5120]{1,0:T(8,128)(2,1)S(1)}, bf16[512,5120]{1,0:T(8,128)(2,1)}, u32[]{:S(2)}) %copy-start) | copy-done | bytes 5242904
  2.5 0.0 copy-start.1
  2.5 1.7 %copy-done.1 = bf16[256,5120]{1,0:T(8,128)(2,1)S(1)} copy-done((bf16[256,5120]{1,0:T(8,128)(2,1)S(1)}, bf16[256,5120]{1,0:T(8,128)(2,1)}, u32[]{:S(2)}) %copy-start.1) | copy-done | bytes 2621464
  4.2 0.0 copy-start.2
  4.2 1.7 %copy-done.2 = bf16[5120,2,128]{2,1,0:T(2,128)(2,1)S(1)} copy-done((bf16[5120,2,128]{2,1,0:T(2,128)(2,1)S(1)}, bf16[5120,2,128]{2,1,0:T(2,128)(2,1)}, u32[]{:S(2)}) %copy-start.2) | copy-done | bytes 2621464
  6.0 0.0 copy-start.3
  6.0 1.0 %copy-done.3 = bf16[16,128,128]{2,1,0:T(8,128)(2,1)S(1)} copy-done((bf16[16,128,128]{2,1,0:T(8,128)(2,1)S(1)}, bf16[16,128,128]{2,1,0:T(8,128)(2,1)}, u32[]{:S(2)}) %copy-start.3) | copy-done | bytes 524312
  7.0 0.0 copy-start.4
  7.0 1.0 %copy-done.4 = bf16[16,128,128]{2,1,0:T(8,128)(2,1)S(1)} copy-done((bf16[16,128,128]{2,1,0:T(8,128)(2,1)S(1)}, bf16[16,128,128]{2,1,0:T(8,128)(2,1)}, u32[]{:S(2)}) %copy-start.4) | copy-done | bytes 524312
  8.1 0.0 copy-start.5
  8.1 1.0 %copy-done.5 = f32[584,128]{1,0:T(8,128)S(1)} copy-done((f32[584,128]{1,0:T(8,128)S(1)}, f32[584,128]{1,0:T(8,128)}, u32[]{:S(2)}) %copy-start.5) | copy-done | bytes 299032
  9.0 0.0 copy-start.6
  9.0 0.7 %copy-done.6 = bf16[4,512]{1,0:T(4,128)(2,1)S(1)} copy-done((bf16[4,512]{1,0:T(4,128)(2,1)S(1)}, bf16[4,512]{1,0:T(4,128)(2,1)}, u32[]{:S(2)}) %copy-start.6) | copy-done | bytes 4120
  9.7 0.0 copy-start.7
  9.7 0.7 %copy-done.7 = s32[4,4]{1,0:T(4,128)S(1)} copy-done((s32[4,4]{1,0:T(4,128)S(1)}, s32[4,4]{1,0:T(4,128)}, u32[]{:S(2)}) %copy-start.7) | copy-done | bytes 88
  10.4 0.0 copy-start.8
  10.4 0.7 %copy-done.8 = f32[128]{0:T(128)S(1)} copy-done((f32[128]{0:T(128)S(1)}, f32[128]{0:T(128)}, u32[]{:S(2)}) %copy-start.8) | copy-done | bytes 536
  11.0 0.0 copy-start.9
  11.0 0.7 %copy-done.9 = s32[128]{0:T(128)S(1)} copy-done((s32[128]{0:T(128)S(1)}, s32[128]{0:T(128)}, u32[]{:S(2)}) %copy-start.9) | copy-done | bytes 536
  11.7 0.0 copy-start.10
  11.7 0.7 %copy-done.10 = s32[128]{0:T(128)S(1)} copy-done((s32[128]{0:T(128)S(1)}, s32[128]{0:T(128)}, u32[]{:S(2)}) %copy-start.10) | copy-done | bytes 536
  12.4 36.0 %shard_map.109 = bf16[4,5120]{1,0:T(4,128)(2,1)S(1)} custom-call(bf16[256,5120]{1,0:T(8,128)(2,1)S(1)} %copy-done.1, bf16[10240,128]{1,0:T(8,128)(2,1)S(1)} %bitcast.6, f32[1,128]{1,0:T(1,128)S(1)} %bitcast.9, bf16[4,512]{1,0:T(4,128)(2,1)S(1)} %copy-done.6, bf16[2048,128]{1,0:T(8,128)(2,1)S(1)} %bitcast.7, bf16[2048,128]{1,0:T(8,128)(2,1)S(1)} %bitcast.8, ...), custom_call_target="tpu_custom_call" | custom-call | flops 1500000000 | bytes 12000000 | tf_op jit(solution)/shard_map/pallas_call | solution.py:383
  48.4 0.6 %copy.13 = bf16[4,5120]{1,0:T(4,128)(2,1)} copy(bf16[4,5120]{1,0:T(4,128)(2,1)S(1)} %shard_map.109) | data formatting | bytes 81920
Async XLA Ops:
  0.0 2.5 %copy-start = (bf16[512,5120]{1,0:T(8,128)(2,1)S(1)}, bf16[512,5120]{1,0:T(8,128)(2,1)}, u32[]{:S(2)}) copy-start(bf16[512,5120]{1,0:T(8,128)(2,1)} %ow_hbm.1) | copy-start | bytes 15728644
  2.5 1.7 %copy-start.1 = (bf16[256,5120]{1,0:T(8,128)(2,1)S(1)}, bf16[256,5120]{1,0:T(8,128)(2,1)}, u32[]{:S(2)}) copy-start(bf16[256,5120]{1,0:T(8,128)(2,1)} %x_hbm.1) | copy-start | bytes 7864324
  4.2 1.7 %copy-start.2 = (bf16[5120,2,128]{2,1,0:T(2,128)(2,1)S(1)}, bf16[5120,2,128]{2,1,0:T(2,128)(2,1)}, u32[]{:S(2)}) copy-start(bf16[5120,2,128]{2,1,0:T(2,128)(2,1)} %param.12) | copy-start | bytes 7864324
  6.0 1.0 %copy-start.3 = (bf16[16,128,128]{2,1,0:T(8,128)(2,1)S(1)}, bf16[16,128,128]{2,1,0:T(8,128)(2,1)}, u32[]{:S(2)}) copy-start(bf16[16,128,128]{2,1,0:T(8,128)(2,1)} %param.15) | copy-start | bytes 1572868
  7.0 1.0 %copy-start.4 = (bf16[16,128,128]{2,1,0:T(8,128)(2,1)S(1)}, bf16[16,128,128]{2,1,0:T(8,128)(2,1)}, u32[]{:S(2)}) copy-start(bf16[16,128,128]{2,1,0:T(8,128)(2,1)} %param.16) | copy-start | bytes 1572868
  8.1 1.0 %copy-start.5 = (f32[584,128]{1,0:T(8,128)S(1)}, f32[584,128]{1,0:T(8,128)}, u32[]{:S(2)}) copy-start(f32[584,128]{1,0:T(8,128)} %constant.2.clone.tab_hbm) | copy-start | bytes 897028
  9.0 0.7 %copy-start.6 = (bf16[4,512]{1,0:T(4,128)(2,1)S(1)}, bf16[4,512]{1,0:T(4,128)(2,1)}, u32[]{:S(2)}) copy-start(bf16[4,512]{1,0:T(4,128)(2,1)} %q_hbm.1) | copy-start | bytes 12292
  9.7 0.7 %copy-start.7 = (s32[4,4]{1,0:T(4,128)S(1)}, s32[4,4]{1,0:T(4,128)}, u32[]{:S(2)}) copy-start(s32[4,4]{1,0:T(4,128)} %pt_hbm.1) | copy-start | bytes 196
  10.4 0.7 %copy-start.8 = (f32[128]{0:T(128)S(1)}, f32[128]{0:T(128)}, u32[]{:S(2)}) copy-start(f32[128]{0:T(128)} %param.13) | copy-start | bytes 1540
  11.0 0.7 %copy-start.9 = (s32[128]{0:T(128)S(1)}, s32[128]{0:T(128)}, u32[]{:S(2)}) copy-start(s32[128]{0:T(128)} %param.18) | copy-start | bytes 1540
  11.7 0.7 %copy-start.10 = (s32[128]{0:T(128)S(1)}, s32[128]{0:T(128)}, u32[]{:S(2)}) copy-start(s32[128]{0:T(128)} %param.19) | copy-start | bytes 1540

commit v2 on v1

--- a/solution.py
+++ b/solution.py
@@ -419,7 +419,7 @@
             pltpu.SemaphoreType.DMA((5,)),
         ],
         compiler_params=pltpu.CompilerParams(
-            collective_id=0, has_side_effects=True, vmem_limit_bytes=40 * 1024 * 1024
+            collective_id=0, has_side_effects=True, vmem_limit_bytes=62 * 1024 * 1024
         ),
         cost_estimate=pl.CostEstimate(
             flops=1_500_000_000, bytes_accessed=12_000_000, transcendentals=200_000

time: 49.4 us -> 37.4 us (0.76)
  local copies, waits for them, and re-layouts: 13 us -> 1.41 us
    unnamed x23 -> x1, local copies, waits for them, and re-layouts: 13 us -> 1.41 us
where the time goes in v2:
time: 37.4 us; the launch traced here: 37.2 us
  Pallas kernels  35.8 us (96%)
  local copies, waits for them, and re-layouts  1.41 us (4%)
    pallas_call x1, Pallas kernels, local(): pl.pallas_call(kernel, out_shape=jax.ShapeDtypeStruct((4, D), bf16), in_s...  35.8 us
    unnamed x1, local copies, waits for them, and re-layouts  1.41 us

profile of v2, /device:TPU:1, one launch (start us, length us, event | category | flops | bytes accessed | tf_op | source)
XLA Modules:
  0.0 37.2 jit_solution(4144066781470847297)
XLA Ops:
  0.0 35.8 %shard_map.109 = bf16[4,5120]{1,0:T(4,128)(2,1)} custom-call(bf16[256,5120]{1,0:T(8,128)(2,1)} %x_hbm.1, bf16[10240,128]{1,0:T(8,128)(2,1)} %bitcast.6, f32[1,128]{1,0:T(1,128)} %bitcast.9, bf16[4,512]{1,0:T(4,128)(2,1)} %q_hbm.1, bf16[2048,128]{1,0:T(8,128)(2,1)} %bitcast.7, bf16[2048,128]{1,0:T(8,128)(2,1)} %bitcast.8, s32[4,4]{1,0:T(4,128)} %pt_hbm.1, ...), custom_call_target="tpu_custom_call" | custom-call | flops 1500000000 | bytes 12000000 | tf_op jit(solution)/shard_map/pallas_call | solution.py:383
  35.8 1.4 %copy.13 = bf16[4,5120]{1,0:T(4,128)(2,1)} copy(bf16[4,5120]{1,0:T(4,128)(2,1)} %shard_map.109) | data formatting | bytes 81920

commit v3 on v2

--- a/solution.py
+++ b/solution.py
@@ -16,7 +16,9 @@
 ROWS = 256
 NC = 5
 DC = D // NC
-COLS = D // T
+COL4 = D // 4
+PC = 256
+NP = COL4 // PC
 MESH = pl.DeviceIdType.MESH
 
 COS0, SIN0, COSB, SINB, FREQ = 0, 256, 512, 544, 576
@@ -32,6 +34,21 @@
     return np.concatenate([np.cos(row), np.sin(row), np.cos(base), np.sin(base), last]).astype(
         np.float32
     )
+
+
+def samp_peer(me, k):
+    dz, dx = k // 4, k % 4
+    dz = 4 + (dz + 1) // 2 * (1 - 2 * (dz % 2))
+    dx = 2 + (dx + 1) // 2 * (1 - 2 * (dx % 2))
+    return lax.rem(me // 8 + dx, 4) * 8 + lax.rem(lax.rem(me, 8) + dz, 8)
+
+
+def tp_peers(mt):
+    for dy in (2, 1, 3, 0):
+        same = lax.rem(mt + 2 * dy, T)
+        if dy:
+            yield same
+        yield same + 1 - 2 * lax.rem(same, 2)
 
 
 def swap_halves(v):
@@ -74,9 +91,8 @@
     st_send,
     st_all,
     tr_v,
-    rs_send,
-    rs_all,
-    ag,
+    tp_send,
+    tp_all,
     small_sem,
     chunk_sem,
     page_sem,
@@ -130,17 +146,14 @@
 
     barrier = pltpu.get_barrier_semaphore()
 
-    @pl.loop(1, S)
+    @pl.loop(0, S - 1)
     def _(k):
         pl.semaphore_signal(
-            barrier, inc=1, device_id={"samp": lax.rem(me + k, S)}, device_id_type=MESH
-        )
-
-    @pl.loop(1, T)
-    def _(k):
-        pl.semaphore_signal(
-            barrier, inc=1, device_id={"tp": lax.rem(mt + k, T)}, device_id_type=MESH
-        )
+            barrier, inc=1, device_id={"samp": samp_peer(me, k)}, device_id_type=MESH
+        )
+
+    for peer in tp_peers(mt):
+        pl.semaphore_signal(barrier, inc=1, device_id={"tp": peer}, device_id_type=MESH)
 
     for copy in small:
         copy.wait()
@@ -172,14 +185,14 @@
 
     pl.semaphore_wait(barrier, S - 1 + T - 1)
 
-    @pl.loop(1, S)
+    @pl.loop(0, S - 1)
     def _(k):
         pltpu.make_async_remote_copy(
             src_ref=q_send,
             dst_ref=q_all.at[me],
             send_sem=send_sem.at[0],
             recv_sem=recv_sem.at[0],
-            device_id={"samp": lax.rem(me + k, S)},
+            device_id={"samp": samp_peer(me, k)},
             device_id_type=MESH,
         ).start()
 
@@ -258,9 +271,9 @@
         st_send[g, 0:1, :] = top[:, g * 128 : (g + 1) * 128]
         st_send[g, 1:2, :] = total[:, g * 128 : (g + 1) * 128]
 
-    @pl.loop(1, S)
+    @pl.loop(0, S - 1)
     def _(k):
-        peer = lax.rem(me + k, S)
+        peer = samp_peer(me, k)
         pltpu.make_async_remote_copy(
             src_ref=o_send.at[peer],
             dst_ref=o_all.at[me],
@@ -323,55 +336,47 @@
     for i in range(S):
         attended = attended + factor[:, i : i + 1] * o_all[i].astype(jnp.float32)
     attended = attended / whole
-    attended = jnp.concatenate(
-        [attended if h == 0 else pltpu.roll(attended, 16 - 4 * h, 0) for h in range(4)], axis=1
-    ).astype(jnp.bfloat16)
+    turned = [attended] + [pltpu.roll(attended, 4 * n, 0) for n in range(1, 4)]
 
     ow_copy.wait()
-
-    @pl.loop(1, T)
-    def _(k):
-        peer = lax.rem(mt + k, T)
-        columns = pl.ds(pl.multiple_of(peer * COLS, COLS), COLS)
-        piece = jnp.dot(attended, ow_v[:, columns], preferred_element_type=jnp.float32)
-        rs_send[peer] = piece[0:4, :]
-        pltpu.make_async_remote_copy(
-            src_ref=rs_send.at[peer],
-            dst_ref=rs_all.at[mt],
-            send_sem=send_sem.at[3],
-            recv_sem=recv_sem.at[3],
-            device_id={"tp": peer},
-            device_id_type=MESH,
-        ).start()
-
-    columns = pl.ds(pl.multiple_of(mt * COLS, COLS), COLS)
-    rs_all[mt] = jnp.dot(attended, ow_v[:, columns], preferred_element_type=jnp.float32)[0:4, :]
+    group = lax.shift_right_logical(lax.broadcasted_iota(jnp.int32, (16, 512), 0), 2)
+    placed = [
+        jnp.where(
+            group == c, jnp.concatenate([turned[(c - h) % 4] for h in range(4)], axis=1), 0.0
+        ).astype(jnp.bfloat16)
+        for c in range(4)
+    ]
+    for p in range(NP):
+        share = sum(
+            jnp.dot(
+                placed[c],
+                ow_v[:, COL4 * c + PC * p : COL4 * c + PC * (p + 1)],
+                preferred_element_type=jnp.float32,
+            )
+            for c in range(4)
+        ).astype(jnp.bfloat16)
+        tp_send[p] = share
+        for peer in tp_peers(mt):
+            pltpu.make_async_remote_copy(
+                src_ref=tp_send.at[p],
+                dst_ref=tp_all.at[mt, p],
+                send_sem=send_sem.at[3],
+                recv_sem=recv_sem.at[3],
+                device_id={"tp": peer},
+                device_id_type=MESH,
+            ).start()
+        tp_all[mt, p] = share
     pltpu.make_async_copy(
-        rs_all.at[pl.ds(0, T - 1)], rs_all.at[pl.ds(0, T - 1)], recv_sem.at[3]
+        tp_all.at[pl.ds(0, T - 1)], tp_all.at[pl.ds(0, T - 1)], recv_sem.at[3]
     ).wait()
-    piece = rs_all[0]
-    for t in range(1, T):
-        piece = piece + rs_all[t]
-    ag[mt] = piece
-
-    @pl.loop(1, T)
-    def _(k):
-        pltpu.make_async_remote_copy(
-            src_ref=ag.at[mt],
-            dst_ref=ag.at[mt],
-            send_sem=send_sem.at[4],
-            recv_sem=recv_sem.at[4],
-            device_id={"tp": lax.rem(mt + k, T)},
-            device_id_type=MESH,
-        ).start()
-
-    pltpu.make_async_copy(
-        ag.at[pl.ds(0, T - 1)], ag.at[pl.ds(0, T - 1)], recv_sem.at[4]
-    ).wait()
-    for t in range(T):
-        out_ref[:, t * COLS : (t + 1) * COLS] = ag[t].astype(jnp.bfloat16)
-
-    for sem, buffer, n in ((0, q_all, S), (1, o_all, S), (2, st_all, S), (3, rs_all, T), (4, ag, T)):
+    for p in range(NP):
+        mixed = sum(tp_all[t, p].astype(jnp.float32) for t in range(T))
+        for c in range(4):
+            out_ref[:, COL4 * c + PC * p : COL4 * c + PC * (p + 1)] = mixed[
+                4 * c : 4 * c + 4, :
+            ].astype(jnp.bfloat16)
+
+    for sem, buffer, n in ((0, q_all, S), (1, o_all, S), (2, st_all, S), (3, tp_all, T)):
         part_ref = buffer.at[pl.ds(0, n - 1)]
         pltpu.make_async_copy(part_ref, part_ref, send_sem.at[sem]).wait()
 
@@ -408,15 +413,14 @@
             V((4, 2, 128), f32),
             V((S, 2, 128), f32),
             V((2, 128, 128), f32),
-            V((T, 4, COLS), f32),
-            V((T, 4, COLS), f32),
-            V((T, 4, COLS), f32),
+            V((NP, 16, PC), bf16),
+            V((T, NP, 16, PC), bf16),
             pltpu.SemaphoreType.DMA((8,)),
             pltpu.SemaphoreType.DMA((2, NC)),
             pltpu.SemaphoreType.DMA((2,)),
             pltpu.SemaphoreType.DMA,
-            pltpu.SemaphoreType.DMA((5,)),
-            pltpu.SemaphoreType.DMA((5,)),
+            pltpu.SemaphoreType.DMA((4,)),
+            pltpu.SemaphoreType.DMA((4,)),
         ],
         compiler_params=pltpu.CompilerParams(
             collective_id=0, has_side_effects=True, vmem_limit_bytes=62 * 1024 * 1024

time: 37.4 us -> 33.2 us (0.89)
  Pallas kernels: 35.8 us -> 31.7 us
    pallas_call x1, Pallas kernels: 35.8 us -> 31.7 us  [local(): pl.pallas_call(kernel, out_shape=jax.ShapeDtypeStruct((4, D), bf16), in_s...]
where the time goes in v3:
time: 33.2 us; the launch traced here: 33.1 us
  Pallas kernels  31.7 us (95%)
  local copies, waits for them, and re-layouts  1.41 us (4%)
    pallas_call x1, Pallas kernels, local(): pl.pallas_call(kernel, out_shape=jax.ShapeDtypeStruct((4, D), bf16), in_s...  31.7 us
    unnamed x1, local copies, waits for them, and re-layouts  1.41 us

profile of v3, /device:TPU:1, one launch (start us, length us, event | category | flops | bytes accessed | tf_op | source)
XLA Modules:
  0.0 33.1 jit_solution(1768490894300435183)
XLA Ops:
  0.0 31.7 %shard_map.109 = bf16[4,5120]{1,0:T(4,128)(2,1)} custom-call(bf16[256,5120]{1,0:T(8,128)(2,1)} %x_hbm.1, bf16[10240,128]{1,0:T(8,128)(2,1)} %bitcast.6, f32[1,128]{1,0:T(1,128)} %bitcast.9, bf16[4,512]{1,0:T(4,128)(2,1)} %q_hbm.1, bf16[2048,128]{1,0:T(8,128)(2,1)} %bitcast.7, bf16[2048,128]{1,0:T(8,128)(2,1)} %bitcast.8, s32[4,4]{1,0:T(4,128)} %pt_hbm.1, ...), custom_call_target="tpu_custom_call" | custom-call | flops 1500000000 | bytes 12000000 | tf_op jit(solution)/shard_map/pallas_call | solution.py:388
  31.7 1.4 %copy.13 = bf16[4,5120]{1,0:T(4,128)(2,1)} copy(bf16[4,5120]{1,0:T(4,128)(2,1)} %shard_map.109) | data formatting | bytes 81920

commit v4 on v3

--- a/solution.py
+++ b/solution.py
@@ -423,23 +423,28 @@
             pltpu.SemaphoreType.DMA((4,)),
         ],
         compiler_params=pltpu.CompilerParams(
-            collective_id=0, has_side_effects=True, vmem_limit_bytes=62 * 1024 * 1024
+            collective_id=0, has_side_effects=True, vmem_limit_bytes=40 * 1024 * 1024
         ),
         cost_estimate=pl.CostEstimate(
             flops=1_500_000_000, bytes_accessed=12_000_000, transcendentals=200_000
         ),
     )(
-        x,
-        w.reshape(2 * D, HD),
-        gain.reshape(1, HD),
-        q,
-        rk.reshape(2048, HD),
-        rv.reshape(2048, HD),
-        pt,
-        div.reshape(1, 128),
-        length.reshape(1, 128),
-        ow,
-        jnp.asarray(rope_table()),
+        *(
+            pltpu.with_memory_space_constraint(operand, pltpu.HBM)
+            for operand in (
+                x,
+                w.reshape(2 * D, HD),
+                gain.reshape(1, HD),
+                q,
+                rk.reshape(2048, HD),
+                rv.reshape(2048, HD),
+                pt,
+                div.reshape(1, 128),
+                length.reshape(1, 128),
+                ow,
+                jnp.asarray(rope_table()),
+            )
+        )
     )
 
 

time: 33.2 us -> 31.8 us (0.958)
  local copies, waits for them, and re-layouts: 1.41 us -> 0.62 us
  Pallas kernels: 31.7 us -> 31.1 us
    unnamed x1, local copies, waits for them, and re-layouts: 1.41 us -> 0.62 us
    pallas_call x1, Pallas kernels: 31.7 us -> 31.1 us  [local(): pl.pallas_call(kernel, out_shape=jax.ShapeDtypeStruct((4, D), bf16), in_s...]
where the time goes in v4:
time: 31.8 us; the launch traced here: 31.7 us
  Pallas kernels  31.1 us (98%)
  local copies, waits for them, and re-layouts  0.62 us (2%)
    pallas_call x1, Pallas kernels, local(): pl.pallas_call(kernel, out_shape=jax.ShapeDtypeStruct((4, D), bf16), in_s...  31.1 us

profile of v4, /device:TPU:1, one launch (start us, length us, event | category | flops | bytes accessed | tf_op | source)
XLA Modules:
  0.0 31.7 jit_solution(11084992656532446984)
XLA Ops:
  0.0 31.1 %shard_map.109 = bf16[4,5120]{1,0:T(4,128)(2,1)S(1)} custom-call(bf16[256,5120]{1,0:T(8,128)(2,1)} %x_hbm.1, bf16[10240,128]{1,0:T(8,128)(2,1)} %bitcast.6, f32[1,128]{1,0:T(1,128)} %bitcast.9, bf16[4,512]{1,0:T(4,128)(2,1)} %q_hbm.1, bf16[2048,128]{1,0:T(8,128)(2,1)} %bitcast.7, bf16[2048,128]{1,0:T(8,128)(2,1)} %bitcast.8, s32[4,4]{1,0:T(4,128)} %pt_hbm.1, ...), custom_call_target="tpu_custom_call" | custom-call | flops 1500000000 | bytes 12000000 | tf_op jit(solution)/shard_map/pallas_call | solution.py:388
  31.1 0.6 %copy.13 = bf16[4,5120]{1,0:T(4,128)(2,1)} copy(bf16[4,5120]{1,0:T(4,128)(2,1)S(1)} %shard_map.109) | data formatting | bytes 81920

commit v5 on v4

--- a/solution.py
+++ b/solution.py
@@ -22,6 +22,14 @@
 MESH = pl.DeviceIdType.MESH
 
 COS0, SIN0, COSB, SINB, FREQ = 0, 256, 512, 544, 576
+STEPX, STEPZ, PLACE = 577, 581, 585
+
+STEPS = sorted(
+    ((dx, dz) for dx in range(4) for dz in range(8)),
+    key=lambda step: (min(step[0], 4 - step[0]) + min(step[1], 8 - step[1]), step),
+)
+BACK = [STEPS.index((-dx % 4, -dz % 8)) for dx, dz in STEPS]
+GROUPS, PER = 4, 8
 
 
 def rope_table():
@@ -29,18 +37,22 @@
     freq = np.concatenate([freq, freq])
     row = np.arange(ROWS, dtype=np.float64)[:, None] * freq
     base = (np.arange(S, dtype=np.float64) * ROWS)[:, None] * freq
-    last = np.zeros((8, HD))
-    last[:] = freq
+    last = np.zeros((16, HD))
+    last[0] = freq
+    for slot in range(S):
+        lanes = slice(slot % PER * 16, slot % PER * 16 + 16)
+        last[STEPX - FREQ + slot // PER, lanes] = STEPS[slot][0]
+        last[STEPZ - FREQ + slot // PER, lanes] = STEPS[slot][1]
+        last[PLACE - FREQ, slot] = BACK[slot] % PER
     return np.concatenate([np.cos(row), np.sin(row), np.cos(base), np.sin(base), last]).astype(
         np.float32
     )
 
 
-def samp_peer(me, k):
-    dz, dx = k // 4, k % 4
-    dz = 4 + (dz + 1) // 2 * (1 - 2 * (dz % 2))
-    dx = 2 + (dx + 1) // 2 * (1 - 2 * (dx % 2))
-    return lax.rem(me // 8 + dx, 4) * 8 + lax.rem(lax.rem(me, 8) + dz, 8)
+def samp_peer(me, slot):
+    dx, dz = STEPS[slot]
+    x = jnp.bitwise_and(lax.shift_right_logical(me, 3) + dx, 3)
+    return x * 8 + jnp.bitwise_and(me + dz, 7)
 
 
 def tp_peers(mt):
@@ -99,9 +111,18 @@
     ow_sem,
     send_sem,
     recv_sem,
+    q_sem,
 ):
     me = lax.axis_index("samp")
     mt = lax.axis_index("tp")
+
+    barrier = pltpu.get_barrier_semaphore()
+    for slot in range(S - 1, 0, -1):
+        pl.semaphore_signal(
+            barrier, inc=1, device_id={"samp": samp_peer(me, slot)}, device_id_type=MESH
+        )
+    for peer in tp_peers(mt):
+        pl.semaphore_signal(barrier, inc=1, device_id={"tp": peer}, device_id_type=MESH)
 
     small = [
         pltpu.make_async_copy(src, dst, small_sem.at[i])
@@ -144,17 +165,6 @@
     ow_copy = pltpu.make_async_copy(ow_hbm, ow_v, ow_sem)
     ow_copy.start()
 
-    barrier = pltpu.get_barrier_semaphore()
-
-    @pl.loop(0, S - 1)
-    def _(k):
-        pl.semaphore_signal(
-            barrier, inc=1, device_id={"samp": samp_peer(me, k)}, device_id_type=MESH
-        )
-
-    for peer in tp_peers(mt):
-        pl.semaphore_signal(barrier, inc=1, device_id={"tp": peer}, device_id_type=MESH)
-
     for copy in small:
         copy.wait()
     row = lax.broadcasted_iota(jnp.int32, (16, HD), 0)
@@ -181,18 +191,17 @@
     q_app = rotate([my_len[i] - 128 * my_div[i] for i in range(4)])
     q_res[...] = rotate(my_len)
     q_send[...] = q_app
-    q_all[me] = q_app
+    q_all[0] = q_app
 
     pl.semaphore_wait(barrier, S - 1 + T - 1)
 
-    @pl.loop(0, S - 1)
-    def _(k):
+    for slot in range(S - 1, 0, -1):
         pltpu.make_async_remote_copy(
             src_ref=q_send,
-            dst_ref=q_all.at[me],
+            dst_ref=q_all.at[BACK[slot]],
             send_sem=send_sem.at[0],
-            recv_sem=recv_sem.at[0],
-            device_id={"samp": samp_peer(me, k)},
+            recv_sem=q_sem.at[BACK[slot] // PER],
+            device_id={"samp": samp_peer(me, slot)},
             device_id_type=MESH,
         ).start()
 
@@ -201,15 +210,18 @@
     low = used - 128 * high
     pair_row = lax.broadcasted_iota(jnp.int32, (16, 128), 0)
     pair = jnp.where(pair_row == 0, high, jnp.where(pair_row == 1, low, 0))
-    e_row = lax.broadcasted_iota(jnp.int32, (128, 512), 0)
-    e_col = lax.broadcasted_iota(jnp.int32, (128, 512), 1)
-    spread = jnp.where(
-        e_row == 4 * lax.shift_right_logical(e_col, 4) + jnp.bitwise_and(e_col, 3), 1.0, 0.0
-    ).astype(jnp.bfloat16)
-    wide = jnp.dot(
-        pair.astype(jnp.float32).astype(jnp.bfloat16), spread, preferred_element_type=jnp.float32
-    )
-    used_wide = (wide[0:1] * 128.0 + wide[1:2]).astype(jnp.int32)
+    pair = pair.astype(jnp.float32).astype(jnp.bfloat16)
+    e_row = lax.broadcasted_iota(jnp.int32, (128, 128), 0)
+    e_col = lax.broadcasted_iota(jnp.int32, (1, 128), 1)
+    used_wide = []
+    for g in range(GROUPS):
+        step_x = tab_v[STEPX + g : STEPX + g + 1, :].astype(jnp.int32)
+        step_z = tab_v[STEPZ + g : STEPZ + g + 1, :].astype(jnp.int32)
+        owner = jnp.bitwise_and(step_x + lax.shift_right_logical(me, 3), 3) * 8
+        owner = owner + jnp.bitwise_and(step_z + me, 7)
+        spread = jnp.where(e_row == 4 * owner + jnp.bitwise_and(e_col, 3), 1.0, 0.0)
+        wide = jnp.dot(pair, spread.astype(jnp.bfloat16), preferred_element_type=jnp.float32)
+        used_wide.append((wide[0:1] * 128.0 + wide[1:2]).astype(jnp.int32))
 
     p_row = lax.broadcasted_iota(jnp.int32, (256, 256), 0)
     p_col = lax.broadcasted_iota(jnp.int32, (256, 256), 1)
@@ -246,53 +258,49 @@
     sin = sin_0 * cos_b + cos_0 * sin_b
     keys = (keys * cos + swap_halves(keys) * sin).astype(jnp.bfloat16)
 
-    pltpu.make_async_copy(
-        q_all.at[pl.ds(0, S - 1)], q_all.at[pl.ds(0, S - 1)], recv_sem.at[0]
-    ).wait()
-    scores = lax.dot_general(
-        keys,
-        q_all[...].reshape(S * 16, HD),
-        (((1,), (1,)), ((), ())),
-        preferred_element_type=jnp.float32,
-    ) * (HD**-0.5)
-    position = lax.broadcasted_iota(jnp.int32, (ROWS, S * 16), 0) + me * ROWS
-    valid = position < used_wide
-    top = jnp.max(jnp.where(valid, scores, FLOOR), axis=0, keepdims=True)
-    weights = jnp.where(valid, jnp.exp(scores - top), 0.0)
-    total = jnp.sum(weights, axis=0, keepdims=True)
-    part = lax.dot_general(
-        weights.astype(jnp.bfloat16),
-        values,
-        (((0,), (0,)), ((), ())),
-        preferred_element_type=jnp.float32,
-    )
-    o_send[...] = part.astype(jnp.bfloat16).reshape(S, 16, HD)
-    for g in range(4):
-        st_send[g, 0:1, :] = top[:, g * 128 : (g + 1) * 128]
-        st_send[g, 1:2, :] = total[:, g * 128 : (g + 1) * 128]
-
-    @pl.loop(0, S - 1)
-    def _(k):
-        peer = samp_peer(me, k)
-        pltpu.make_async_remote_copy(
-            src_ref=o_send.at[peer],
-            dst_ref=o_all.at[me],
-            send_sem=send_sem.at[1],
-            recv_sem=recv_sem.at[1],
-            device_id={"samp": peer},
-            device_id_type=MESH,
-        ).start()
-        pltpu.make_async_remote_copy(
-            src_ref=st_send.at[peer // 8],
-            dst_ref=st_all.at[me],
-            send_sem=send_sem.at[2],
-            recv_sem=recv_sem.at[2],
-            device_id={"samp": peer},
-            device_id_type=MESH,
-        ).start()
-
-    o_all[me] = o_send[me]
-    st_all[me] = st_send[me // 8]
+    position = lax.broadcasted_iota(jnp.int32, (ROWS, PER * 16), 0) + me * ROWS
+    for g in range(GROUPS):
+        first = 1 if g == 0 else PER * g
+        fresh = q_all.at[pl.ds(first, PER * (g + 1) - first)]
+        pltpu.make_async_copy(fresh, fresh, q_sem.at[g]).wait()
+        scores = lax.dot_general(
+            keys,
+            q_all[PER * g : PER * (g + 1)].reshape(PER * 16, HD),
+            (((1,), (1,)), ((), ())),
+            preferred_element_type=jnp.float32,
+        ) * (HD**-0.5)
+        valid = position < used_wide[g]
+        top = jnp.max(jnp.where(valid, scores, FLOOR), axis=0, keepdims=True)
+        weights = jnp.where(valid, jnp.exp(scores - top), 0.0)
+        total = jnp.sum(weights, axis=0, keepdims=True)
+        part = lax.dot_general(
+            weights.astype(jnp.bfloat16),
+            values,
+            (((0,), (0,)), ((), ())),
+            preferred_element_type=jnp.float32,
+        ).astype(jnp.bfloat16)
+        o_send[PER * g : PER * (g + 1)] = part.reshape(PER, 16, HD)
+        st_send[g, 0:1, :] = top
+        st_send[g, 1:2, :] = total
+        for slot in range(PER * (g + 1) - 1, first - 1, -1):
+            pltpu.make_async_remote_copy(
+                src_ref=st_send.at[g],
+                dst_ref=st_all.at[BACK[slot]],
+                send_sem=send_sem.at[2],
+                recv_sem=recv_sem.at[1],
+                device_id={"samp": samp_peer(me, slot)},
+                device_id_type=MESH,
+            ).start()
+            pltpu.make_async_remote_copy(
+                src_ref=o_send.at[slot],
+                dst_ref=o_all.at[BACK[slot]],
+                send_sem=send_sem.at[1],
+                recv_sem=recv_sem.at[0],
+                device_id={"samp": samp_peer(me, slot)},
+                device_id_type=MESH,
+            ).start()
+    o_all[0] = o_send[0]
+    st_all[0] = st_send[0]
 
     for copy in pages:
         copy.wait()
@@ -316,18 +324,21 @@
     )
 
     pltpu.make_async_copy(
-        st_all.at[pl.ds(0, S - 1)], st_all.at[pl.ds(0, S - 1)], recv_sem.at[2]
+        st_all.at[pl.ds(0, S - 1)], st_all.at[pl.ds(0, S - 1)], recv_sem.at[1]
     ).wait()
     pltpu.make_async_copy(
-        o_all.at[pl.ds(0, S - 1)], o_all.at[pl.ds(0, S - 1)], recv_sem.at[1]
+        o_all.at[pl.ds(0, S - 1)], o_all.at[pl.ds(0, S - 1)], recv_sem.at[0]
     ).wait()
     tops = jnp.concatenate([st_all[:, 0, :], jnp.full((128 - S, 128), FLOOR, jnp.float32)], axis=0)
     totals = jnp.concatenate([st_all[:, 1, :], jnp.zeros((128 - S, 128), jnp.float32)], axis=0)
     tr_v[0] = tops.T
     tr_v[1] = totals.T
-    mine = pl.multiple_of(16 * lax.rem(me, 8), 16)
-    tops = tr_v[0, pl.ds(mine, 16), :]
-    totals = tr_v[1, pl.ds(mine, 16), :]
+    place = tab_v[PLACE : PLACE + 1, :]
+    tops, totals = tr_v[0, 0:16, :], tr_v[1, 0:16, :]
+    for n in range(1, PER):
+        here = jnp.broadcast_to(place, (16, HD)) == float(n)
+        tops = jnp.where(here, tr_v[0, 16 * n : 16 * n + 16, :], tops)
+        totals = jnp.where(here, tr_v[1, 16 * n : 16 * n + 16, :], totals)
     highest = jnp.maximum(jnp.max(tops, axis=1, keepdims=True), res_top)
     factor = jnp.exp(tops - highest)
     res_factor = jnp.exp(res_top - highest)
@@ -361,13 +372,13 @@
                 src_ref=tp_send.at[p],
                 dst_ref=tp_all.at[mt, p],
                 send_sem=send_sem.at[3],
-                recv_sem=recv_sem.at[3],
+                recv_sem=recv_sem.at[2],
                 device_id={"tp": peer},
                 device_id_type=MESH,
             ).start()
         tp_all[mt, p] = share
     pltpu.make_async_copy(
-        tp_all.at[pl.ds(0, T - 1)], tp_all.at[pl.ds(0, T - 1)], recv_sem.at[3]
+        tp_all.at[pl.ds(0, T - 1)], tp_all.at[pl.ds(0, T - 1)], recv_sem.at[2]
     ).wait()
     for p in range(NP):
         mixed = sum(tp_all[t, p].astype(jnp.float32) for t in range(T))
@@ -404,7 +415,7 @@
             V((1, 128), i32),
             V((1, 128), i32),
             V((512, D), bf16),
-            V((584, HD), f32),
+            V((592, HD), f32),
             V((16, HD), bf16),
             V((16, HD), bf16),
             V((S, 16, HD), bf16),
@@ -420,7 +431,8 @@
             pltpu.SemaphoreType.DMA((2,)),
             pltpu.SemaphoreType.DMA,
             pltpu.SemaphoreType.DMA((4,)),
-            pltpu.SemaphoreType.DMA((4,)),
+            pltpu.SemaphoreType.DMA((3,)),
+            pltpu.SemaphoreType.DMA((GROUPS,)),
         ],
         compiler_params=pltpu.CompilerParams(
             collective_id=0, has_side_effects=True, vmem_limit_bytes=40 * 1024 * 1024

time: 31.8 us -> 31.7 us (level)
  no operation moved by 1% of the time
where the time goes in v5:
time: 31.7 us
  Pallas kernels  31 us (98%)
  local copies, waits for them, and re-layouts  0.62 us (2%)
    pallas_call x1, Pallas kernels, local(): pl.pallas_call(kernel, out_shape=jax.ShapeDtypeStruct((4, D), bf16), in_s...  31 us

profile of v5, /device:TPU:1, one launch (start us, length us, event | category | flops | bytes accessed | tf_op | source)
XLA Modules:
  0.0 31.7 jit_solution(9061820006707088989)
XLA Ops:
  0.0 31.0 %shard_map.109 = bf16[4,5120]{1,0:T(4,128)(2,1)S(1)} custom-call(bf16[256,5120]{1,0:T(8,128)(2,1)} %x_hbm.1, bf16[10240,128]{1,0:T(8,128)(2,1)} %bitcast.6, f32[1,128]{1,0:T(1,128)} %bitcast.9, bf16[4,512]{1,0:T(4,128)(2,1)} %q_hbm.1, bf16[2048,128]{1,0:T(8,128)(2,1)} %bitcast.7, bf16[2048,128]{1,0:T(8,128)(2,1)} %bitcast.8, s32[4,4]{1,0:T(4,128)} %pt_hbm.1, ...), custom_call_target="tpu_custom_call" | custom-call | flops 1500000000 | bytes 12000000 | tf_op jit(solution)/shard_map/pallas_call | solution.py:399
  31.0 0.6 %copy.13 = bf16[4,5120]{1,0:T(4,128)(2,1)} copy(bf16[4,5120]{1,0:T(4,128)(2,1)S(1)} %shard_map.109) | data formatting | bytes 81920

commit v6 on v5

--- a/solution.py
+++ b/solution.py
@@ -43,7 +43,7 @@
         lanes = slice(slot % PER * 16, slot % PER * 16 + 16)
         last[STEPX - FREQ + slot // PER, lanes] = STEPS[slot][0]
         last[STEPZ - FREQ + slot // PER, lanes] = STEPS[slot][1]
-        last[PLACE - FREQ, slot] = BACK[slot] % PER
+        last[PLACE - FREQ, slot] = BACK[slot] % 4
     return np.concatenate([np.cos(row), np.sin(row), np.cos(base), np.sin(base), last]).astype(
         np.float32
     )
@@ -112,6 +112,7 @@
     send_sem,
     recv_sem,
     q_sem,
+    tp_sem,
 ):
     me = lax.axis_index("samp")
     mt = lax.axis_index("tp")
@@ -153,9 +154,8 @@
         )
         for c in range(NC)
     ]
-    for c in range(NC):
-        w_copies[c].start()
-        x_copies[c].start()
+    for copy in w_copies + x_copies:
+        copy.start()
     pages = [
         pltpu.make_async_copy(rk_hbm, rk_v, page_sem.at[0]),
         pltpu.make_async_copy(rv_hbm, rv_v, page_sem.at[1]),
@@ -192,18 +192,6 @@
     q_res[...] = rotate(my_len)
     q_send[...] = q_app
     q_all[0] = q_app
-
-    pl.semaphore_wait(barrier, S - 1 + T - 1)
-
-    for slot in range(S - 1, 0, -1):
-        pltpu.make_async_remote_copy(
-            src_ref=q_send,
-            dst_ref=q_all.at[BACK[slot]],
-            send_sem=send_sem.at[0],
-            recv_sem=q_sem.at[BACK[slot] // PER],
-            device_id={"samp": samp_peer(me, slot)},
-            device_id_type=MESH,
-        ).start()
 
     used = len_v[...] - 128 * div_v[...]
     high = lax.shift_right_logical(used, 7)
@@ -228,7 +216,6 @@
     perm = jnp.where(
         p_col == jnp.where(p_row < 128, 2 * p_row, 2 * p_row - 255), 1.0, 0.0
     ).astype(jnp.bfloat16)
-    acc = jnp.zeros((ROWS, 256), jnp.float32)
     for c in range(NC):
         w_copies[c].wait()
         for i in range(c * DC // 256, (c + 1) * DC // 256):
@@ -240,6 +227,21 @@
             wd[pl.ds(i * 256, 128), 128:256] = apart[128:256, 0:128]
             wd[pl.ds(i * 256 + 128, 128), 0:128] = apart[0:128, 128:256]
             wd[pl.ds(i * 256 + 128, 128), 128:256] = apart[128:256, 128:256]
+
+    pl.semaphore_wait(barrier, S - 1 + T - 1)
+
+    for slot in range(S - 1, 0, -1):
+        pltpu.make_async_remote_copy(
+            src_ref=q_send,
+            dst_ref=q_all.at[BACK[slot]],
+            send_sem=send_sem.at[0],
+            recv_sem=q_sem.at[BACK[slot] // PER],
+            device_id={"samp": samp_peer(me, slot)},
+            device_id_type=MESH,
+        ).start()
+
+    acc = jnp.zeros((ROWS, 256), jnp.float32)
+    for c in range(NC):
         x_copies[c].wait()
         acc = acc + jnp.dot(
             x_v[:, c * DC : (c + 1) * DC],
@@ -259,7 +261,7 @@
     keys = (keys * cos + swap_halves(keys) * sin).astype(jnp.bfloat16)
 
     position = lax.broadcasted_iota(jnp.int32, (ROWS, PER * 16), 0) + me * ROWS
-    for g in range(GROUPS):
+    for g in reversed(range(GROUPS)):
         first = 1 if g == 0 else PER * g
         fresh = q_all.at[pl.ds(first, PER * (g + 1) - first)]
         pltpu.make_async_copy(fresh, fresh, q_sem.at[g]).wait()
@@ -280,11 +282,12 @@
             preferred_element_type=jnp.float32,
         ).astype(jnp.bfloat16)
         o_send[PER * g : PER * (g + 1)] = part.reshape(PER, 16, HD)
-        st_send[g, 0:1, :] = top
-        st_send[g, 1:2, :] = total
+        for half in (0, 1):
+            lanes = slice(64 * half, 64 * half + 64)
+            st_send[2 * g + half] = jnp.concatenate([top[:, lanes], total[:, lanes]], axis=1)
         for slot in range(PER * (g + 1) - 1, first - 1, -1):
             pltpu.make_async_remote_copy(
-                src_ref=st_send.at[g],
+                src_ref=st_send.at[slot // 4],
                 dst_ref=st_all.at[BACK[slot]],
                 send_sem=send_sem.at[2],
                 recv_sem=recv_sem.at[1],
@@ -326,27 +329,26 @@
     pltpu.make_async_copy(
         st_all.at[pl.ds(0, S - 1)], st_all.at[pl.ds(0, S - 1)], recv_sem.at[1]
     ).wait()
-    pltpu.make_async_copy(
-        o_all.at[pl.ds(0, S - 1)], o_all.at[pl.ds(0, S - 1)], recv_sem.at[0]
-    ).wait()
-    tops = jnp.concatenate([st_all[:, 0, :], jnp.full((128 - S, 128), FLOOR, jnp.float32)], axis=0)
-    totals = jnp.concatenate([st_all[:, 1, :], jnp.zeros((128 - S, 128), jnp.float32)], axis=0)
-    tr_v[0] = tops.T
-    tr_v[1] = totals.T
-    place = tab_v[PLACE : PLACE + 1, :]
-    tops, totals = tr_v[0, 0:16, :], tr_v[1, 0:16, :]
-    for n in range(1, PER):
-        here = jnp.broadcast_to(place, (16, HD)) == float(n)
-        tops = jnp.where(here, tr_v[0, 16 * n : 16 * n + 16, :], tops)
-        totals = jnp.where(here, tr_v[1, 16 * n : 16 * n + 16, :], totals)
+    tr_v[...] = jnp.concatenate(
+        [st_all[:, 0, :], jnp.zeros((128 - S, 128), jnp.float32)], axis=0
+    ).T
+    place = jnp.broadcast_to(tab_v[PLACE : PLACE + 1, :], (16, HD))
+    tops, totals = tr_v[0:16, :], tr_v[64:80, :]
+    for n in range(1, 4):
+        tops = jnp.where(place == float(n), tr_v[16 * n : 16 * n + 16, :], tops)
+        totals = jnp.where(place == float(n), tr_v[16 * n + 64 : 16 * n + 80, :], totals)
+    tops = jnp.where(lane < S, tops, FLOOR)
     highest = jnp.maximum(jnp.max(tops, axis=1, keepdims=True), res_top)
     factor = jnp.exp(tops - highest)
     res_factor = jnp.exp(res_top - highest)
     whole = jnp.sum(factor * totals, axis=1, keepdims=True) + res_factor * res_total
-    attended = res_part * res_factor
+    pltpu.make_async_copy(
+        o_all.at[pl.ds(0, S - 1)], o_all.at[pl.ds(0, S - 1)], recv_sem.at[0]
+    ).wait()
+    attended = [res_part * res_factor] + [jnp.zeros((16, HD), jnp.float32)] * 3
     for i in range(S):
-        attended = attended + factor[:, i : i + 1] * o_all[i].astype(jnp.float32)
-    attended = attended / whole
+        attended[i % 4] = attended[i % 4] + factor[:, i : i + 1] * o_all[i].astype(jnp.float32)
+    attended = (attended[0] + attended[1] + attended[2] + attended[3]) / whole
     turned = [attended] + [pltpu.roll(attended, 4 * n, 0) for n in range(1, 4)]
 
     ow_copy.wait()
@@ -370,25 +372,28 @@
         for peer in tp_peers(mt):
             pltpu.make_async_remote_copy(
                 src_ref=tp_send.at[p],
-                dst_ref=tp_all.at[mt, p],
+                dst_ref=tp_all.at[p, mt],
                 send_sem=send_sem.at[3],
-                recv_sem=recv_sem.at[2],
+                recv_sem=tp_sem.at[p],
                 device_id={"tp": peer},
                 device_id_type=MESH,
             ).start()
-        tp_all[mt, p] = share
-    pltpu.make_async_copy(
-        tp_all.at[pl.ds(0, T - 1)], tp_all.at[pl.ds(0, T - 1)], recv_sem.at[2]
-    ).wait()
+        tp_all[p, mt] = share
     for p in range(NP):
-        mixed = sum(tp_all[t, p].astype(jnp.float32) for t in range(T))
+        fresh = tp_all.at[p, pl.ds(0, T - 1)]
+        pltpu.make_async_copy(fresh, fresh, tp_sem.at[p]).wait()
+        mixed = sum(tp_all[p, t].astype(jnp.float32) for t in range(T))
         for c in range(4):
             out_ref[:, COL4 * c + PC * p : COL4 * c + PC * (p + 1)] = mixed[
                 4 * c : 4 * c + 4, :
             ].astype(jnp.bfloat16)
 
-    for sem, buffer, n in ((0, q_all, S), (1, o_all, S), (2, st_all, S), (3, tp_all, T)):
-        part_ref = buffer.at[pl.ds(0, n - 1)]
+    for sem, part_ref in (
+        (0, q_all.at[pl.ds(0, S - 1)]),
+        (1, o_all.at[pl.ds(0, S - 1)]),
+        (2, st_all.at[pl.ds(0, S - 1)]),
+        (3, tp_all.at[:, pl.ds(0, T - 1)]),
+    ):
         pltpu.make_async_copy(part_ref, part_ref, send_sem.at[sem]).wait()
 
 
@@ -421,18 +426,19 @@
             V((S, 16, HD), bf16),
             V((S, 16, HD), bf16),
             V((S, 16, HD), bf16),
-            V((4, 2, 128), f32),
-            V((S, 2, 128), f32),
-            V((2, 128, 128), f32),
+            V((2 * GROUPS, 1, 128), f32),
+            V((S, 1, 128), f32),
+            V((128, 128), f32),
             V((NP, 16, PC), bf16),
-            V((T, NP, 16, PC), bf16),
+            V((NP, T, 16, PC), bf16),
             pltpu.SemaphoreType.DMA((8,)),
             pltpu.SemaphoreType.DMA((2, NC)),
             pltpu.SemaphoreType.DMA((2,)),
             pltpu.SemaphoreType.DMA,
             pltpu.SemaphoreType.DMA((4,)),
-            pltpu.SemaphoreType.DMA((3,)),
+            pltpu.SemaphoreType.DMA((2,)),
             pltpu.SemaphoreType.DMA((GROUPS,)),
+            pltpu.SemaphoreType.DMA((NP,)),
         ],
         compiler_params=pltpu.CompilerParams(
             collective_id=0, has_side_effects=True, vmem_limit_bytes=40 * 1024 * 1024

time: 31.7 us -> 31.3 us (0.987)
  Pallas kernels: 31 us -> 30.6 us
    pallas_call x1, Pallas kernels: 31 us -> 30.6 us  [local(): pl.pallas_call(kernel, out_shape=jax.ShapeDtypeStruct((4, D), bf16), in_s...]
where the time goes in v6:
time: 31.3 us; the launch traced here: 31.2 us
  Pallas kernels  30.6 us (98%)
  local copies, waits for them, and re-layouts  0.62 us (2%)
    pallas_call x1, Pallas kernels, local(): pl.pallas_call(kernel, out_shape=jax.ShapeDtypeStruct((4, D), bf16), in_s...  30.6 us

profile of v6, /device:TPU:1, one launch (start us, length us, event | category | flops | bytes accessed | tf_op | source)
XLA Modules:
  0.0 31.2 jit_solution(8765507301716049162)
XLA Ops:
  0.0 30.6 %shard_map.109 = bf16[4,5120]{1,0:T(4,128)(2,1)S(1)} custom-call(bf16[256,5120]{1,0:T(8,128)(2,1)} %x_hbm.1, bf16[10240,128]{1,0:T(8,128)(2,1)} %bitcast.6, f32[1,128]{1,0:T(1,128)} %bitcast.9, bf16[4,512]{1,0:T(4,128)(2,1)} %q_hbm.1, bf16[2048,128]{1,0:T(8,128)(2,1)} %bitcast.7, bf16[2048,128]{1,0:T(8,128)(2,1)} %bitcast.8, s32[4,4]{1,0:T(4,128)} %pt_hbm.1, ...), custom_call_target="tpu_custom_call" | custom-call | flops 1500000000 | bytes 12000000 | tf_op jit(solution)/shard_map/pallas_call | solution.py:404
  30.6 0.6 %copy.13 = bf16[4,5120]{1,0:T(4,128)(2,1)} copy(bf16[4,5120]{1,0:T(4,128)(2,1)S(1)} %shard_map.109) | data formatting | bytes 81920

commit v7 on v6

--- a/solution.py
+++ b/solution.py
@@ -17,7 +17,7 @@
 NC = 5
 DC = D // NC
 COL4 = D // 4
-PC = 256
+PC = 640
 NP = COL4 // PC
 MESH = pl.DeviceIdType.MESH
 
@@ -193,6 +193,18 @@
     q_send[...] = q_app
     q_all[0] = q_app
 
+    pl.semaphore_wait(barrier, S - 1 + T - 1)
+
+    for slot in range(S - 1, 0, -1):
+        pltpu.make_async_remote_copy(
+            src_ref=q_send,
+            dst_ref=q_all.at[BACK[slot]],
+            send_sem=send_sem.at[0],
+            recv_sem=q_sem.at[BACK[slot] // PER],
+            device_id={"samp": samp_peer(me, slot)},
+            device_id_type=MESH,
+        ).start()
+
     used = len_v[...] - 128 * div_v[...]
     high = lax.shift_right_logical(used, 7)
     low = used - 128 * high
@@ -227,18 +239,6 @@
             wd[pl.ds(i * 256, 128), 128:256] = apart[128:256, 0:128]
             wd[pl.ds(i * 256 + 128, 128), 0:128] = apart[0:128, 128:256]
             wd[pl.ds(i * 256 + 128, 128), 128:256] = apart[128:256, 128:256]
-
-    pl.semaphore_wait(barrier, S - 1 + T - 1)
-
-    for slot in range(S - 1, 0, -1):
-        pltpu.make_async_remote_copy(
-            src_ref=q_send,
-            dst_ref=q_all.at[BACK[slot]],
-            send_sem=send_sem.at[0],
-            recv_sem=q_sem.at[BACK[slot] // PER],
-            device_id={"samp": samp_peer(me, slot)},
-            device_id_type=MESH,
-        ).start()
 
     acc = jnp.zeros((ROWS, 256), jnp.float32)
     for c in range(NC):

time: 31.3 us -> 31.4 us (level)
  no operation moved by 1% of the time
where the time goes in v7:
time: 31.4 us; the launch traced here: 31.3 us
  Pallas kernels  30.7 us (98%)
  local copies, waits for them, and re-layouts  0.62 us (2%)
    pallas_call x1, Pallas kernels, local(): pl.pallas_call(kernel, out_shape=jax.ShapeDtypeStruct((4, D), bf16), in_s...  30.7 us

profile of v7, /device:TPU:1, one launch (start us, length us, event | category | flops | bytes accessed | tf_op | source)
XLA Modules:
  0.0 31.3 jit_solution(10713036489370253248)
XLA Ops:
  0.0 30.7 %shard_map.109 = bf16[4,5120]{1,0:T(4,128)(2,1)S(1)} custom-call(bf16[256,5120]{1,0:T(8,128)(2,1)} %x_hbm.1, bf16[10240,128]{1,0:T(8,128)(2,1)} %bitcast.6, f32[1,128]{1,0:T(1,128)} %bitcast.9, bf16[4,512]{1,0:T(4,128)(2,1)} %q_hbm.1, bf16[2048,128]{1,0:T(8,128)(2,1)} %bitcast.7, bf16[2048,128]{1,0:T(8,128)(2,1)} %bitcast.8, s32[4,4]{1,0:T(4,128)} %pt_hbm.1, ...), custom_call_target="tpu_custom_call" | custom-call | flops 1500000000 | bytes 12000000 | tf_op jit(solution)/shard_map/pallas_call | solution.py:404
  30.7 0.6 %copy.13 = bf16[4,5120]{1,0:T(4,128)(2,1)} copy(bf16[4,5120]{1,0:T(4,128)(2,1)S(1)} %shard_map.109) | data formatting | bytes 81920

commit v8 on v7

--- a/solution.py
+++ b/solution.py
@@ -275,13 +275,6 @@
         top = jnp.max(jnp.where(valid, scores, FLOOR), axis=0, keepdims=True)
         weights = jnp.where(valid, jnp.exp(scores - top), 0.0)
         total = jnp.sum(weights, axis=0, keepdims=True)
-        part = lax.dot_general(
-            weights.astype(jnp.bfloat16),
-            values,
-            (((0,), (0,)), ((), ())),
-            preferred_element_type=jnp.float32,
-        ).astype(jnp.bfloat16)
-        o_send[PER * g : PER * (g + 1)] = part.reshape(PER, 16, HD)
         for half in (0, 1):
             lanes = slice(64 * half, 64 * half + 64)
             st_send[2 * g + half] = jnp.concatenate([top[:, lanes], total[:, lanes]], axis=1)
@@ -294,6 +287,14 @@
                 device_id={"samp": samp_peer(me, slot)},
                 device_id_type=MESH,
             ).start()
+        part = lax.dot_general(
+            weights.astype(jnp.bfloat16),
+            values,
+            (((0,), (0,)), ((), ())),
+            preferred_element_type=jnp.float32,
+        ).astype(jnp.bfloat16)
+        o_send[PER * g : PER * (g + 1)] = part.reshape(PER, 16, HD)
+        for slot in range(PER * (g + 1) - 1, first - 1, -1):
             pltpu.make_async_remote_copy(
                 src_ref=o_send.at[slot],
                 dst_ref=o_all.at[BACK[slot]],

time: 31.4 us -> 31.1 us (level)
  no operation moved by 1% of the time
where the time goes in v8:
time: 31.1 us
  Pallas kernels  30.4 us (98%)
  local copies, waits for them, and re-layouts  0.62 us (2%)
    pallas_call x1, Pallas kernels, local(): pl.pallas_call(kernel, out_shape=jax.ShapeDtypeStruct((4, D), bf16), in_s...  30.4 us

profile of v8, /device:TPU:1, one launch (start us, length us, event | category | flops | bytes accessed | tf_op | source)
XLA Modules:
  0.0 31.1 jit_solution(16776947670802135172)
XLA Ops:
  0.0 30.4 %shard_map.109 = bf16[4,5120]{1,0:T(4,128)(2,1)S(1)} custom-call(bf16[256,5120]{1,0:T(8,128)(2,1)} %x_hbm.1, bf16[10240,128]{1,0:T(8,128)(2,1)} %bitcast.6, f32[1,128]{1,0:T(1,128)} %bitcast.9, bf16[4,512]{1,0:T(4,128)(2,1)} %q_hbm.1, bf16[2048,128]{1,0:T(8,128)(2,1)} %bitcast.7, bf16[2048,128]{1,0:T(8,128)(2,1)} %bitcast.8, s32[4,4]{1,0:T(4,128)} %pt_hbm.1, ...), custom_call_target="tpu_custom_call" | custom-call | flops 1500000000 | bytes 12000000 | tf_op jit(solution)/shard_map/pallas_call | solution.py:405
  30.4 0.6 %copy.13 = bf16[4,5120]{1,0:T(4,128)(2,1)} copy(bf16[4,5120]{1,0:T(4,128)(2,1)S(1)} %shard_map.109) | data formatting | bytes 81920

commit v9 on v7

--- a/solution.py
+++ b/solution.py
@@ -26,7 +26,7 @@
 
 STEPS = sorted(
     ((dx, dz) for dx in range(4) for dz in range(8)),
-    key=lambda step: (min(step[0], 4 - step[0]) + min(step[1], 8 - step[1]), step),
+    key=lambda step: (min(step[0], 4 - step[0]) + 2 * min(step[1], 8 - step[1]), step),
 )
 BACK = [STEPS.index((-dx % 4, -dz % 8)) for dx, dz in STEPS]
 GROUPS, PER = 4, 8

time: 31.4 us -> 31.3 us (level)
  no operation moved by 1% of the time
where the time goes in v9:
time: 31.3 us; the launch traced here: 31.2 us
  Pallas kernels  30.6 us (98%)
  local copies, waits for them, and re-layouts  0.62 us (2%)
    pallas_call x1, Pallas kernels, local(): pl.pallas_call(kernel, out_shape=jax.ShapeDtypeStruct((4, D), bf16), in_s...  30.6 us

profile of v9, /device:TPU:1, one launch (start us, length us, event | category | flops | bytes accessed | tf_op | source)
XLA Modules:
  0.0 31.2 jit_solution(3638107851258259368)
XLA Ops:
  0.0 30.6 %shard_map.109 = bf16[4,5120]{1,0:T(4,128)(2,1)S(1)} custom-call(bf16[256,5120]{1,0:T(8,128)(2,1)} %x_hbm.1, bf16[10240,128]{1,0:T(8,128)(2,1)} %bitcast.6, f32[1,128]{1,0:T(1,128)} %bitcast.9, bf16[4,512]{1,0:T(4,128)(2,1)} %q_hbm.1, bf16[2048,128]{1,0:T(8,128)(2,1)} %bitcast.7, bf16[2048,128]{1,0:T(8,128)(2,1)} %bitcast.8, s32[4,4]{1,0:T(4,128)} %pt_hbm.1, ...), custom_call_target="tpu_custom_call" | custom-call | flops 1500000000 | bytes 12000000 | tf_op jit(solution)/shard_map/pallas_call | solution.py:404
  30.6 0.6 %copy.13 = bf16[4,5120]{1,0:T(4,128)(2,1)} copy(bf16[4,5120]{1,0:T(4,128)(2,1)S(1)} %shard_map.109) | data formatting | bytes 81920
